TPU v7x, 128 devices: a whole 4x4x4 slice. The times are simulated.
128 devices in a mesh: dp: 32 (over z, x, core), db: 4 (over y).
Axes of the slice: x: 4, y: 4, z: 4, core: 2. Of those that a mesh axis runs over, the one named last changes fastest.
Arguments:
- queries: bfloat16 [18432, 4096], P('dp', 'db'), may hold values from -100 to 100
- cotangent: bfloat16 [18432, 4096], P('dp', 'db'), may hold values from -6 to 6
- db_states: bfloat16 [1024, 128, 896], P('dp', 'db'), may hold values from -6 to 6
- key_weight: bfloat16 [896, 4096], P(None, 'db'), may hold values from -0.1875 to 0.1875
- value_weight: bfloat16 [896, 4096], P(None, 'db'), may hold values from -0.1875 to 0.1875
- conv_kernel: float32 [3, 896], replicated, may hold values from -2.5 to 2.5
- nbr_owner: int32 [288, 2], P('dp'), may hold values from 0 to 31, all different within a row; in each aligned block of 9 rows (0 to 8, 9 to 17, ...) at most 2 rows name the same one
- nbr_row: int32 [288, 2], P('dp'), may hold values from 0 to 31
Outputs:
- attended: bfloat16 [18432, 4096], P('dp', 'db')
- grad_queries: bfloat16 [18432, 4096], P('dp', 'db')
- grad_states: float32 [1024, 128, 896], P('dp', 'db')
- grad_key_weight: float32 [896, 4096], P(None, 'db')
- grad_value_weight: float32 [896, 4096], P(None, 'db')
- grad_kernel: float32 [3, 896], replicated
Inputs may be any that keep to these rules, and one draw needn't show every extreme that they name: `nbr_owner`: in the 9 spans of one index of dp no owner is named more than 2 times, a bound that some block reaches; the 2 neighbours of a span have different owners.
All inputs are finite; a program needn't handle non-finite values.
Results may differ from a plain program's by a relative error of at most 0.035.
The roundings to bfloat16 on the way count: a program that leaves them out, or rounds other values in their place, can miss the bound.
Values may be sent and summed in bfloat16 or wider, within the bound.
A program may use at most 192 MiB of HBM per device.

v0:
```python
import math
import jax
import jax.numpy as jnp
from jax import lax
from jax.sharding import PartitionSpec as P

HD = 128
ENC = 896
SPAN = 64
NBR = 2
NLEN = 128
KW = 3


def extended(block, sides, width):
    for axis, dim in sides:
        count = lax.axis_size(axis)
        forward = [(i, i + 1) for i in range(count - 1)]
        backward = [(target, source) for source, target in forward]
        low = lax.ppermute(
            lax.slice_in_dim(block, block.shape[dim] - width, None, axis=dim), axis, forward
        )
        high = lax.ppermute(lax.slice_in_dim(block, 0, width, axis=dim), axis, backward)
        block = jnp.concatenate([low, block, high], axis=dim)
    return block


def conv_apply(padded, kernel, length):
    summed = kernel[0] * padded[:, 0:length, :].astype(jnp.float32)
    for offset in range(1, KW):
        summed = summed + kernel[offset] * padded[:, offset : offset + length, :].astype(
            jnp.float32
        )
    return summed


def conv_adjoint(grad_padded, kernel, length):
    final_tap = KW - 1
    summed = kernel[0] * grad_padded[:, final_tap : final_tap + length, :]
    for offset in range(1, KW):
        begin = final_tap - offset
        summed = summed + kernel[offset] * grad_padded[:, begin : begin + length, :]
    return summed


def taps_gradient(grad_mixed, padded, length):
    return jnp.stack(
        [
            jnp.sum(
                grad_mixed * padded[:, offset : offset + length, :].astype(jnp.float32), axis=(0, 1)
            )
            for offset in range(KW)
        ]
    )


def shards(
    queries, cotangent, db_states, key_weight, value_weight, conv_kernel, nbr_owner, nbr_row
):
    half_taps = (KW - 1) // 2
    score_scale = 1.0 / math.sqrt(HD)
    owners = lax.axis_size("dp")
    span_count = nbr_owner.shape[0]
    request_count = span_count * NBR
    capacity = max(2, (request_count + owners - 1) // owners)
    quarter = db_states.shape[1]
    local_blocks = db_states.shape[0]
    slots_total = owners * capacity
    local_width = key_weight.shape[1]
    local_heads = local_width // HD
    owner_flat = nbr_owner.reshape(request_count)
    row_flat = nbr_row.reshape(request_count)
    positions = jnp.arange(request_count, dtype=jnp.int32)
    same_owner = owner_flat[:, None] == owner_flat[None, :]
    earlier = positions[:, None] > positions[None, :]
    slot_index = jnp.sum(jnp.logical_and(same_owner, earlier).astype(jnp.int32), axis=1)
    target = owner_flat * capacity + slot_index
    slot_hits = target[:, None] == jnp.arange(slots_total, dtype=jnp.int32)[None, :]
    used_slot = jnp.any(slot_hits, axis=0)
    row_sent = jnp.sum(jnp.where(slot_hits, row_flat[:, None], 0), axis=0)
    row_table = jnp.where(used_slot, row_sent, -1).reshape(owners, capacity)
    slot_matrix = slot_hits.astype(jnp.bfloat16)
    states_flat = db_states.reshape(local_blocks, quarter * ENC)
    asked = lax.all_to_all(row_table, "dp", split_axis=0, concat_axis=0, tiled=True)
    sources = asked.shape[0]
    items = asked.shape[1]
    asked_flat = asked.reshape(sources * items)
    picker = (asked_flat[:, None] == jnp.arange(local_blocks, dtype=jnp.int32)[None, :]).astype(
        jnp.bfloat16
    )
    fetched = jnp.dot(picker, states_flat, preferred_element_type=jnp.float32).astype(jnp.bfloat16)
    fetched = fetched.reshape(sources, items, quarter, ENC)
    replied = lax.all_to_all(fetched, "dp", split_axis=0, concat_axis=0, tiled=True)
    received = jnp.dot(
        slot_matrix, replied.reshape(slots_total, quarter * ENC), preferred_element_type=jnp.float32
    )
    received = received.astype(jnp.bfloat16).reshape(request_count, quarter, ENC)
    padded_part = extended(received, (("db", 1),), half_taps)
    mixed_part = conv_apply(padded_part, conv_kernel, quarter).astype(jnp.bfloat16)
    mixed = lax.all_gather(mixed_part, "db", axis=1, tiled=True)
    mixed_flat = mixed.reshape(request_count * NLEN, ENC)
    keys = jnp.dot(mixed_flat, key_weight, preferred_element_type=jnp.float32).astype(jnp.bfloat16)
    values = jnp.dot(mixed_flat, value_weight, preferred_element_type=jnp.float32).astype(
        jnp.bfloat16
    )
    key_heads = keys.reshape(span_count, NBR * NLEN, local_heads, HD)
    value_heads = values.reshape(span_count, NBR * NLEN, local_heads, HD)
    query_heads = queries.reshape(span_count, SPAN, local_heads, HD)
    grad_heads = cotangent.reshape(span_count, SPAN, local_heads, HD)
    scores = (
        jnp.einsum("cqhd,ckhd->chqk", query_heads, key_heads, preferred_element_type=jnp.float32)
        * score_scale
    )
    highest = jnp.max(scores, axis=-1, keepdims=True)
    expo = jnp.exp(scores - highest)
    probs = expo / jnp.sum(expo, axis=-1, keepdims=True)
    probs_b = probs.astype(jnp.bfloat16)
    attended = jnp.einsum(
        "chqk,ckhd->cqhd", probs_b, value_heads, preferred_element_type=jnp.float32
    ).astype(jnp.bfloat16)
    grad_probs = jnp.einsum(
        "cqhd,ckhd->chqk", grad_heads, value_heads, preferred_element_type=jnp.float32
    )
    grad_values = jnp.einsum(
        "chqk,cqhd->ckhd", probs_b, grad_heads, preferred_element_type=jnp.float32
    ).astype(jnp.bfloat16)
    inner = jnp.sum(grad_probs * probs, axis=-1, keepdims=True)
    grad_scores = (score_scale * probs * (grad_probs - inner)).astype(jnp.bfloat16)
    grad_query = jnp.einsum(
        "chqk,ckhd->cqhd", grad_scores, key_heads, preferred_element_type=jnp.float32
    ).astype(jnp.bfloat16)
    grad_keys = jnp.einsum(
        "chqk,cqhd->ckhd", grad_scores, query_heads, preferred_element_type=jnp.float32
    ).astype(jnp.bfloat16)
    keys_flat = grad_keys.reshape(request_count * NLEN, local_width)
    values_flat = grad_values.reshape(request_count * NLEN, local_width)
    key_term = jnp.einsum("ne,nf->ef", mixed_flat, keys_flat, preferred_element_type=jnp.float32)
    value_term = jnp.einsum(
        "ne,nf->ef", mixed_flat, values_flat, preferred_element_type=jnp.float32
    )
    grad_mixed = jnp.einsum("nf,ef->ne", keys_flat, key_weight, preferred_element_type=jnp.float32)
    grad_mixed = grad_mixed + jnp.einsum(
        "nf,ef->ne", values_flat, value_weight, preferred_element_type=jnp.float32
    )
    grad_mixed = grad_mixed.reshape(request_count, NLEN, ENC)
    grad_mixed_part = lax.psum_scatter(grad_mixed, "db", scatter_dimension=1, tiled=True)
    grad_padded = extended(grad_mixed_part, (("db", 1),), half_taps)
    grad_raw = conv_adjoint(grad_padded, conv_kernel, quarter)
    taps_term = taps_gradient(grad_mixed_part, padded_part, quarter)
    grad_raw_b = grad_raw.astype(jnp.bfloat16).reshape(request_count, quarter * ENC)
    grad_send = jnp.einsum(
        "ns,nf->sf", slot_matrix, grad_raw_b, preferred_element_type=jnp.float32
    ).astype(jnp.bfloat16)
    grad_send = grad_send.reshape(owners, capacity, quarter, ENC)
    grad_back = lax.all_to_all(grad_send, "dp", split_axis=0, concat_axis=0, tiled=True)
    asked_flat = asked.reshape(slots_total)
    picker_back = (
        jnp.arange(local_blocks, dtype=jnp.int32)[:, None] == asked_flat[None, :]
    ).astype(jnp.bfloat16)
    grad_states = jnp.dot(
        picker_back,
        grad_back.reshape(slots_total, quarter * ENC),
        preferred_element_type=jnp.float32,
    )
    grad_states = grad_states.reshape(local_blocks, quarter, ENC)
    grad_key_weight, grad_value_weight = lax.psum((key_term, value_term), "dp")
    grad_kernel = lax.psum(taps_term, ("dp", "db"))
    return (
        attended.reshape(span_count * SPAN, local_width),
        grad_query.reshape(span_count * SPAN, local_width),
        grad_states,
        grad_key_weight,
        grad_value_weight,
        grad_kernel,
    )


def solution(mesh):
    return jax.shard_map(
        shards,
        mesh=mesh,
        in_specs=(
            P("dp", "db"),
            P("dp", "db"),
            P("dp", "db", None),
            P(None, "db"),
            P(None, "db"),
            P(),
            P("dp", None),
            P("dp", None),
        ),
        out_specs=(
            P("dp", "db"),
            P("dp", "db"),
            P("dp", "db", None),
            P(None, "db"),
            P(None, "db"),
            P(),
        ),
        check_vma=False,
    )
```

profile of v0, /device:TPU:6, one launch (start us, length us, event | category | flops | bytes accessed | tf_op | source)
XLA Modules:
  0.0 488.2 jit_solution(10462257573725515154)
XLA Ops:
  7.2 0.9 copy.58
  8.2 0.2 convert_reduce_fusion
  8.5 0.8 copy.59
  9.4 0.7 select_n.21
  10.1 8.4 %all-to-all-start = ((s32[32,1,2]{2,1,0:T(1,128)}), s32[32,1,2]{2,1,0:T(1,128)S(1)}, u32[]{:S(2)}, u32[]{:S(2)}) async-start(s32[32,1,2]{2,1,0:T(1,128)} %bitcast), calls=%async_computation | async-start | bytes 32768 | tf_op jit(solution)/shard_map/all_to_all | solution.py:84
  18.6 3.3 copy.76
  21.9 2.1 all-to-all-done
  24.0 0.5 broadcast.51
  24.5 0.7 reduce.9
  25.3 2.6 convolution_convert_fusion.1
  28.0 0.6 copy.77
  28.5 48.2 %all_to_all.16 = bf16[32,2,32,896]{3,2,1,0:T(8,128)(2,1)S(1)} all-to-all(bf16[32,2,32,896]{3,2,1,0:T(8,128)(2,1)S(1)} %bitcast.131), channel_id=1, replica_groups=mesh['dp'=32,'db'=4] {'dp'}, dimensions={0} | all-to-all | bytes 7340032 | tf_op jit(solution)/shard_map/all_to_all | solution.py:93
  76.8 1.4 copy.78
  78.2 0.7 convolution_convert_fusion.2
  78.8 0.2 copy.79
  79.1 3.5 collective-permute-start
  82.6 1.3 collective-permute-start.1
  84.1 0.9 collective-permute-done
  85.0 4.3 collective-permute-done.1
  89.2 1.8 fusion.36
  91.1 0.2 reduce-scatter.2.cloned.1.call-start
  91.3 1.6 copy.81
  92.9 2.6 copy.84
  95.5 42.6 %all-gather.2.cloned.1.call-done = bf16[18,128,896]{2,1,0:T(8,128)(2,1)} async-done(((bf16[18,32,896]{2,1,0:T(8,128)(2,1)}), bf16[18,128,896]{2,1,0:T(8,128)(2,1)}) %all-gather.2.cloned.1.call-update) | async-done | bytes 4128784 | tf_op jit(solution)/shard_map/all_gather | solution.py:100
  138.1 7.4 %fusion.33 = bf16[288,8,8,128]{3,1,2,0:T(8,128)(2,1)S(1)} fusion(bf16[2304,896]{1,0:T(8,128)(2,1)} %bitcast.159, bf16[896,1024]{1,0:T(8,128)(2,1)S(1)} %copy-done), kind=kOutput, calls=%fused_computation.50 | convolution fusion | flops 4230217728 | bytes 10682368 | tf_op jit(solution)/shard_map/dot_general | solution.py:102
  145.6 1.3 copy.80
  146.9 0.9 copy-done.16
  147.8 0.6 copy-done.17
  148.3 5.5 %fusion.32 = bf16[288,8,8,128]{3,1,2,0:T(8,128)(2,1)S(1)} fusion(bf16[2304,896]{1,0:T(8,128)(2,1)S(1)} %bitcast.162, bf16[896,1024]{1,0:T(8,128)(2,1)S(1)} %copy-done.17), kind=kOutput, calls=%fused_computation.49 | convolution fusion | flops 4230217728 | bytes 10682368 | tf_op jit(solution)/shard_map/dot_general | solution.py:103
  153.8 3.4 copy.82
  157.2 1.8 fusion.23
  158.9 3.6 fusion.82
  162.5 15.7 %convert_bitcast_fusion = bf16[9,256,8,128]{3,1,2,0:T(8,128)(2,1)} fusion(bf16[9,64,8,128]{3,2,1,0:T(8,128)(2,1)} %bitcast.157, f32[9,8,64]{2,1,0:T(8,128)S(1)} %get-tuple-element.43, f32[9,8,256,64]{2,3,1,0:T(8,128)} %copy-done.5), kind=kOutput, calls=%fused_computation.23 | convolution fusion | flops 310252288 | bytes 10635264 | tf_op jit(solution)/shard_map/chqk,cqhd->ckhd/dot_general | solution.py:124
  178.2 5.7 %copy.72 = bf16[9,256,8,128]{3,2,1,0:T(8,128)(2,1)S(1)} copy(bf16[9,256,8,128]{3,1,2,0:T(8,128)(2,1)} %convert_bitcast_fusion) | data formatting | bytes 9437184 | tf_op jit(solution)/shard_map/convert_element_type | solution.py:126
  184.0 5.8 %fusion.8 = (f32[9,8,64]{2,1,0:T(8,128)S(1)}, f32[9,8,256,64]{2,3,1,0:T(8,128)S(1)}) fusion(f32[9,8,64,256]{3,2,1,0:T(8,128)S(1)} %copy-done.4, f32[9,8,64]{2,1,0:T(8,128)S(1)} %get-tuple-element.43, bf16[9,64,8,128]{3,2,1,0:T(8,128)(2,1)S(1)} %bitcast.158, bf16[9,256,8,128]{3,2,1,0:T(8,128)(2,1)} %bitcast.146), kind=kOutput, calls=%fused_computation.16 | convolution fusion | flops 305524224 | bytes 15372288 | tf_op jit(solution)/shard_map/cqhd,ckhd->chqk/dot_general | solution.py:121
  189.8 1.5 fusion.10
  191.3 1.4 copy-done.3
  192.7 1.7 convert_bitcast_fusion.1
  194.4 3.3 copy.70
  197.7 7.3 %fusion.6 = f32[2304,896]{1,0:T(8,128)} fusion(bf16[896,1024]{1,0:T(8,128)(2,1)S(1)} %copy-done, bf16[288,8,8,128]{3,2,1,0:T(8,128)(2,1)S(1)} %bitcast.150), kind=kOutput, calls=%fused_computation.12 | convolution fusion | flops 4227858432 | bytes 14811136 | tf_op jit(solution)/shard_map/nf,ef->ne/dot_general | solution.py:141
  205.0 9.5 %convolution_add_fusion = f32[2304,896]{1,0:T(8,128)} fusion(f32[2304,896]{1,0:T(8,128)} %fusion.6, bf16[896,1024]{1,0:T(8,128)(2,1)S(1)} %copy-done.18, bf16[288,8,8,128]{3,2,1,0:T(8,128)(2,1)S(1)} %bitcast.148), kind=kOutput, calls=%fused_computation.4 | convolution fusion | flops 4229922816 | bytes 23068672 | tf_op jit(solution)/shard_map/nf,ef->ne/dot_general | solution.py:142
  214.4 79.9 %reduce-scatter.2.cloned.1.call-done = f32[18,32,896]{2,1,0:T(8,128)} async-done(((f32[18,128,896]{2,1,0:T(8,128)}), f32[18,32,896]{2,1,0:T(8,128)}) %reduce-scatter.2.cloned.1.call-update) | async-done | bytes 2064400 | tf_op jit(solution)/shard_map/reduce_scatter | solution.py:146
  294.4 1.3 fusion.80
  295.6 1.3 collective-permute-start.2
  297.0 5.3 %collective-permute-start.3 = (f32[18,1,896]{2,1,0:T(1,128)S(1)}, f32[18,1,896]{2,1,0:T(1,128)S(1)}, u32[]{:S(2)}, u32[]{:S(2)}) collective-permute-start(f32[18,1,896]{2,1,0:T(1,128)S(1)} %get-tuple-element.40), channel_id=1, source_target_pairs={{0,1},{1,2},{2,3},{4,5},{5,6},{6,7},{8,9},{9,10},{10,11},{12,13},{... | collective-permute-start | bytes 193544 | tf_op jit(solution)/shard_map/ppermute | solution.py:20
  302.3 9.9 %fusion.4 = f32[896,1024]{1,0:T(8,128)} fusion(bf16[2304,896]{1,0:T(8,128)(2,1)} %bitcast.160, bf16[288,8,8,128]{3,2,1,0:T(8,128)(2,1)} %bitcast.151), kind=kOutput, calls=%fused_computation.10 | convolution fusion | flops 4227858432 | bytes 12517376 | tf_op jit(solution)/shard_map/ne,nf->ef/dot_general | solution.py:137
  312.2 2.2 fusion.37
  314.6 0.4 copy.88
  315.0 1.2 convolution_convert_fusion
  316.2 2.4 copy.89
  318.6 7.6 %all-to-all-start.2 = ((bf16[32,2,32,896]{3,2,1,0:T(8,128)(2,1)}), bf16[32,2,32,896]{3,2,1,0:T(8,128)(2,1)}, u32[]{:S(2)}, u32[]{:S(2)}) async-start(bf16[32,2,32,896]{3,2,1,0:T(8,128)(2,1)} %bitcast.130), calls=%async_computation.3 | async-start | bytes 7340032 | tf_op jit(solution)/shard_map/all_to_all | solution.py:155
  326.2 0.2 all-reduce.3.cloned.1.call-start
  326.5 9.9 %fusion.1 = f32[896,1024]{1,0:T(8,128)} fusion(bf16[2304,896]{1,0:T(8,128)(2,1)} %bitcast.161, bf16[288,8,8,128]{3,2,1,0:T(8,128)(2,1)} %bitcast.149), kind=kOutput, calls=%fused_computation.7 | convolution fusion | flops 4227858432 | bytes 12517376 | tf_op jit(solution)/shard_map/ne,nf->ef/dot_general | solution.py:138
  336.4 3.8 fusion.54
  340.2 0.8 copy.68
  341.1 14.0 %fusion.51 = bf16[9,64,8,128]{3,1,2,0:T(8,128)(2,1)S(1)} fusion(bf16[9,256,8,128]{3,2,1,0:T(8,128)(2,1)} %bitcast.147, f32[9,8,64]{2,1,0:T(8,128)S(1)} %get-tuple-element.43, f32[9,8,256,64]{2,3,1,0:T(8,128)} %copy-done.5), kind=kOutput, calls=%fused_computation.66 | convolution fusion | flops 308482816 | bytes 10635264 | tf_op jit(solution)/shard_map/chqk,ckhd->cqhd/dot_general | solution.py:118
  355.0 1.0 copy.64
  356.1 2.0 copy_bitcast_fusion
  358.1 73.3 %psum.23 = f32[3,896]{1,0:T(4,128)} all-reduce(f32[3,896]{1,0:T(4,128)S(1)} %pad_maximum_fusion.4), channel_id=1, replica_groups=mesh['dp'=32,'db'=4] {'dp','db'}, use_global_device_ids=true, to_apply=%region_12.13 | all-reduce | flops 2688 | bytes 21504 | tf_op jit(solution)/shard_map/psum | solution.py:167
  431.4 4.4 fusion.26
  435.8 4.0 copy.74
  439.8 35.3 %all-reduce.3.cloned.1.call-done = (f32[896,1024]{1,0:T(8,128)}, f32[896,1024]{1,0:T(8,128)}) async-done(((f32[896,1024]{1,0:T(8,128)}, f32[896,1024]{1,0:T(8,128)}), (f32[896,1024]{1,0:T(8,128)}, f32[896,1024]{1,0:T(8,128)})) %all-reduce.3.cloned.1.call-update) | async-done | bytes 7340048 | tf_op jit(solution)/shard_map/psum | solution.py:166
  475.1 4.5 copy.146
  479.6 1.8 copy.147
  (57 shorter events, 1.0 us)
Async XLA Ops:
  7.2 131.0 %copy-start = (bf16[896,1024]{1,0:T(8,128)(2,1)S(1)}, bf16[896,1024]{1,0:T(8,128)(2,1)}, u32[]{:S(2)}) copy-start(bf16[896,1024]{1,0:T(8,128)(2,1)} %param.11) | copy-start | bytes 5505028
  10.1 13.9 %all-to-all-start = ((s32[32,1,2]{2,1,0:T(1,128)}), s32[32,1,2]{2,1,0:T(1,128)S(1)}, u32[]{:S(2)}, u32[]{:S(2)}) async-start(s32[32,1,2]{2,1,0:T(1,128)} %bitcast), calls=%async_computation | async-start | bytes 32768 | tf_op jit(solution)/shard_map/all_to_all | solution.py:84
  18.5 119.6 %all-gather.2.cloned.1.call-start = ((), (), s32[]{:S(2)}) async-start(), calls=%async_computation.4 | async-start | bytes 5160960 | tf_op jit(solution)/shard_map/all_gather | solution.py:100
  78.1 5.8 %copy-start.15 = (f32[3,896]{1,0:T(4,128)S(1)}, f32[3,896]{1,0:T(4,128)}, u32[]{:S(2)}) copy-start(f32[3,896]{1,0:T(4,128)} %param.13) | copy-start | bytes 32260
  79.0 5.0 %copy-start.8 = (bf16[3,8,32,896]{3,2,1,0:T(8,128)(2,1)}, bf16[3,8,32,896]{3,2,1,0:T(8,128)(2,1)S(1)}, u32[]{:S(2)}) copy-start(bf16[3,8,32,896]{3,2,1,0:T(8,128)(2,1)S(1)} %copy.79) | copy-start | bytes 4128772
  79.1 5.9 %collective-permute-start = (bf16[18,1,896]{2,1,0:T(2,128)(2,1)S(1)}, bf16[18,1,896]{2,1,0:T(2,128)(2,1)S(1)}, u32[]{:S(2)}, u32[]{:S(2)}) collective-permute-start(bf16[18,1,896]{2,1,0:T(2,128)(2,1)S(1)} %get-tuple-element.41), channel_id=1, source_target_pairs={{0,1},{1,2},{2,3},{4,5},{5,6},{6,7},{8,9},{9,10},{10,11},{12,13},{... | collective-permute-start | bytes 96776 | tf_op jit(solution)/shard_map/ppermute | solution.py:20
  82.6 6.6 %collective-permute-start.1 = (bf16[18,1,896]{2,1,0:T(2,128)(2,1)S(1)}, bf16[18,1,896]{2,1,0:T(2,128)(2,1)S(1)}, u32[]{:S(2)}, u32[]{:S(2)}) collective-permute-start(bf16[18,1,896]{2,1,0:T(2,128)(2,1)S(1)} %get-tuple-element.42), channel_id=1, source_target_pairs={{1,0},{2,1},{3,2},{5,4},{6,5},{7,6},{9,8},{10,9},{11,10},{13,12},{... | collective-permute-start | bytes 96776 | tf_op jit(solution)/shard_map/ppermute | solution.py:23
  84.1 5.2 %copy-start.6 = (bf16[18,32,896]{2,1,0:T(8,128)(2,1)}, bf16[18,32,896]{2,1,0:T(8,128)(2,1)S(1)}, u32[]{:S(2)}) copy-start(bf16[18,32,896]{2,1,0:T(8,128)(2,1)S(1)} %slice.57) | copy-start | bytes 3096580
  91.1 203.2 %reduce-scatter.2.cloned.1.call-start = ((), (), s32[]{:S(2)}) async-start(), calls=%async_computation.5 | async-start | bytes 10321920 | tf_op jit(solution)/shard_map/reduce_scatter | solution.py:146
  145.6 2.2 copy-start.16
  145.6 2.7 copy-start.17
  148.3 8.8 %copy-start.2 = (bf16[288,8,8,128]{3,2,1,0:T(8,128)(2,1)}, bf16[288,8,8,128]{3,2,1,0:T(8,128)(2,1)S(1)}, u32[]{:S(2)}) copy-start(bf16[288,8,8,128]{3,2,1,0:T(8,128)(2,1)S(1)} %copy.80) | copy-start | bytes 14155780
  158.9 3.6 copy-start.5
  178.2 5.8 %copy-start.4 = (f32[9,8,64,256]{3,2,1,0:T(8,128)S(1)}, f32[9,8,64,256]{3,2,1,0:T(8,128)}, u32[]{:S(2)}) copy-start(f32[9,8,64,256]{3,2,1,0:T(8,128)} %get-tuple-element.44) | copy-start | bytes 14155780
  178.2 5.8 %copy-start.14 = (bf16[72,8,8,128]{3,2,1,0:T(8,128)(2,1)S(1)}, bf16[72,8,8,128]{3,2,1,0:T(8,128)(2,1)}, u32[]{:S(2)}) copy-start(bf16[72,8,8,128]{3,2,1,0:T(8,128)(2,1)} %copy.84) | copy-start | bytes 3538948
  183.9 21.0 %copy-start.10 = (bf16[9,256,8,128]{3,2,1,0:T(8,128)(2,1)}, bf16[9,256,8,128]{3,2,1,0:T(8,128)(2,1)S(1)}, u32[]{:S(2)}) copy-start(bf16[9,256,8,128]{3,2,1,0:T(8,128)(2,1)S(1)} %copy.72) | copy-start | bytes 14155780
  191.3 1.4 copy-start.3
  197.7 7.3 %copy-start.11 = (bf16[9,256,8,128]{3,2,1,0:T(8,128)(2,1)}, bf16[9,256,8,128]{3,2,1,0:T(8,128)(2,1)S(1)}, u32[]{:S(2)}) copy-start(bf16[9,256,8,128]{3,2,1,0:T(8,128)(2,1)S(1)} %copy.70) | copy-start | bytes 14155780
  197.7 7.3 %copy-start.18 = (bf16[896,1024]{1,0:T(8,128)(2,1)S(1)}, bf16[896,1024]{1,0:T(8,128)(2,1)}, u32[]{:S(2)}) copy-start(bf16[896,1024]{1,0:T(8,128)(2,1)} %param.12) | copy-start | bytes 5505028
  295.6 16.5 %collective-permute-start.2 = (f32[18,1,896]{2,1,0:T(1,128)S(1)}, f32[18,1,896]{2,1,0:T(1,128)S(1)}, u32[]{:S(2)}, u32[]{:S(2)}) collective-permute-start(f32[18,1,896]{2,1,0:T(1,128)S(1)} %get-tuple-element.39), channel_id=1, source_target_pairs={{1,0},{2,1},{3,2},{5,4},{6,5},{7,6},{9,8},{10,9},{11,10},{13,12},{... | collective-permute-start | bytes 193544 | tf_op jit(solution)/shard_map/ppermute | solution.py:23
  296.9 15.2 %copy-start.7 = (bf16[18,32,896]{2,1,0:T(8,128)(2,1)S(1)}, bf16[18,32,896]{2,1,0:T(8,128)(2,1)}, u32[]{:S(2)}) copy-start(bf16[18,32,896]{2,1,0:T(8,128)(2,1)} %copy-done.6) | copy-start | bytes 3096580
  297.0 15.2 %copy-start.9 = (bf16[3,8,32,896]{3,2,1,0:T(8,128)(2,1)S(1)}, bf16[3,8,32,896]{3,2,1,0:T(8,128)(2,1)}, u32[]{:S(2)}) copy-start(bf16[3,8,32,896]{3,2,1,0:T(8,128)(2,1)} %copy-done.8) | copy-start | bytes 4128772
  297.0 15.2 %copy-start.13 = (f32[18,32,896]{2,1,0:T(8,128)S(1)}, f32[18,32,896]{2,1,0:T(8,128)}, u32[]{:S(2)}) copy-start(f32[18,32,896]{2,1,0:T(8,128)} %reduce-scatter.2.cloned.1.call-done) | copy-start | bytes 6193156
  297.0 15.2 %collective-permute-start.3 = (f32[18,1,896]{2,1,0:T(1,128)S(1)}, f32[18,1,896]{2,1,0:T(1,128)S(1)}, u32[]{:S(2)}, u32[]{:S(2)}) collective-permute-start(f32[18,1,896]{2,1,0:T(1,128)S(1)} %get-tuple-element.40), channel_id=1, source_target_pairs={{0,1},{1,2},{2,3},{4,5},{5,6},{6,7},{8,9},{9,10},{10,11},{12,13},{... | collective-permute-start | bytes 193544 | tf_op jit(solution)/shard_map/ppermute | solution.py:20
  318.6 112.8 %all-to-all-start.2 = ((bf16[32,2,32,896]{3,2,1,0:T(8,128)(2,1)}), bf16[32,2,32,896]{3,2,1,0:T(8,128)(2,1)}, u32[]{:S(2)}, u32[]{:S(2)}) async-start(bf16[32,2,32,896]{3,2,1,0:T(8,128)(2,1)} %bitcast.130), calls=%async_computation.3 | async-start | bytes 7340032 | tf_op jit(solution)/shard_map/all_to_all | solution.py:155
  326.2 148.8 %all-reduce.3.cloned.1.call-start = ((), (), s32[]{:S(2)}) async-start(), calls=%async_computation.6 | async-start | bytes 14680064 | tf_op jit(solution)/shard_map/psum | solution.py:166
  475.1 4.5 copy-start.12
  475.1 6.4 %copy-start.1 = (bf16[896,1024]{1,0:T(8,128)(2,1)S(1)}, bf16[896,1024]{1,0:T(8,128)(2,1)}, u32[]{:S(2)}) copy-start(bf16[896,1024]{1,0:T(8,128)(2,1)} %param.11) | copy-start | bytes 5505028
Sparse Core Ops, SparseCore 0:
  91.2 46.8 all-gather.1
  214.6 79.7 reduce-scatter.1
  336.5 138.5 all-reduce.2
where the time goes:
time: 494 us; the launch traced here: 488 us
  waiting for transfers between devices  165 us (33%)
  blocking collectives  122 us (25%)
  matrix products  101 us (20%)
  local copies, waits for them, and re-layouts  48.1 us (10%)
  starting transfers between devices  27.8 us (6%)
  between operations  14.4 us (3%)
  other arithmetic  10.2 us (2%)
    reduce_scatter x1, waiting for transfers between devices, shards(): lax.psum_scatter(grad_mixed, 'db', scatter_dimension=1, tiled=True)  79.9 us
    psum x1, blocking collectives, shards(): grad_kernel = lax.psum(taps_term, ('dp', 'db'))  73.3 us
    all_to_all x1, blocking collectives, shards(): lax.all_to_all(fetched, 'dp', split_axis=0, concat_axis=0, tiled=True)  48.2 us
    all_gather x1, waiting for transfers between devices, shards(): mixed = lax.all_gather(mixed_part, 'db', axis=1, tiled=True)  42.6 us
    psum x1, waiting for transfers between devices, shards(): grad_key_weight, grad_value_weight = lax.psum((key_term, value_term), 'dp')  35.3 us
    unnamed x54, local copies, waits for them, and re-layouts  32.2 us
    dot_general x1, matrix products, shards(): jnp.einsum('chqk,cqhd->ckhd', probs_b, grad_heads, preferred_element_type...  15.7 us
    dot_general x1, matrix products, shards(): jnp.einsum('chqk,ckhd->cqhd', probs_b, value_heads, preferred_element_typ...  14 us
  transfers between devices with their start and end apart: 9, of which 6 were waited for; matrix products, arithmetic and copies ran while one was open for 12% of the time, Pallas kernels for 0%

commit v1 on v0

--- a/solution.py
+++ b/solution.py
@@ -164,7 +164,7 @@
     )
     grad_states = grad_states.reshape(local_blocks, quarter, ENC)
     grad_key_weight, grad_value_weight = lax.psum((key_term, value_term), "dp")
-    grad_kernel = lax.psum(taps_term, ("dp", "db"))
+    grad_kernel = jnp.sum(lax.all_gather(taps_term, ("dp", "db")), axis=0)
     return (
         attended.reshape(span_count * SPAN, local_width),
         grad_query.reshape(span_count * SPAN, local_width),

time: 494 us -> 538 us (1.089)
  waiting for transfers between devices: 165 us -> 276 us
  blocking collectives: 122 us -> 48.2 us
  other arithmetic: 10.2 us -> 17.4 us
    psum x1, waiting for transfers between devices: 35.3 us -> 112 us  [shards(): grad_key_weight, grad_value_weight = lax.psum((key_term, value_term), 'dp')]
    psum x1 -> x0, blocking collectives: 73.3 us -> none  [shards(): grad_kernel = lax.psum(taps_term, ('dp', 'db'))]
    all_gather x0 -> x1, waiting for transfers between devices: none -> 33 us  [shards(): grad_kernel = jnp.sum(lax.all_gather(taps_term, ('dp', 'db')), axis=0)]
  transfers between devices with their start and end apart: 9 -> 10, of which waited for: 6 -> 9; matrix products, arithmetic and copies ran while one was open for 12% -> 12% of each run, Pallas kernels for 0% -> 0%
where the time goes in v1:
time: 538 us; the launch traced here: 532 us
  waiting for transfers between devices  276 us (51%)
  matrix products  100 us (19%)
  blocking collectives  48.2 us (9%)
  local copies, waits for them, and re-layouts  48.1 us (9%)
  starting transfers between devices  27.1 us (5%)
  other arithmetic  17.4 us (3%)
  between operations  14.4 us (3%)
    psum x1, waiting for transfers between devices, shards(): grad_key_weight, grad_value_weight = lax.psum((key_term, value_term), 'dp')  112 us
    reduce_scatter x1, waiting for transfers between devices, shards(): lax.psum_scatter(grad_mixed, 'db', scatter_dimension=1, tiled=True)  79.9 us
    all_to_all x1, blocking collectives, shards(): lax.all_to_all(fetched, 'dp', split_axis=0, concat_axis=0, tiled=True)  48.2 us
    all_gather x1, waiting for transfers between devices, shards(): mixed = lax.all_gather(mixed_part, 'db', axis=1, tiled=True)  42.6 us
    all_gather x1, waiting for transfers between devices, shards(): grad_kernel = jnp.sum(lax.all_gather(taps_term, ('dp', 'db')), axis=0)  33 us
    unnamed x54, local copies, waits for them, and re-layouts  32.2 us
    dot_general x1, matrix products, shards(): jnp.einsum('chqk,cqhd->ckhd', probs_b, grad_heads, preferred_element_type...  15.7 us
    dot_general x1, matrix products, shards(): jnp.einsum('chqk,ckhd->cqhd', probs_b, value_heads, preferred_element_typ...  13.3 us
  transfers between devices with their start and end apart: 10, of which 9 were waited for; matrix products, arithmetic and copies ran while one was open for 12% of the time, Pallas kernels for 0%

profile of v1, /device:TPU:6, one launch (start us, length us, event | category | flops | bytes accessed | tf_op | source)
XLA Modules:
  0.0 532.0 jit_solution(7261440808703379059)
XLA Ops:
  7.2 0.9 copy.58
  8.5 0.8 copy.59
  9.4 0.7 select_n.21
  10.1 8.4 %all-to-all-start = ((s32[32,1,2]{2,1,0:T(1,128)}), s32[32,1,2]{2,1,0:T(1,128)S(1)}, u32[]{:S(2)}, u32[]{:S(2)}) async-start(s32[32,1,2]{2,1,0:T(1,128)} %bitcast), calls=%async_computation | async-start | bytes 32768 | tf_op jit(solution)/shard_map/all_to_all | solution.py:84
  18.6 3.3 copy.76
  21.9 2.1 all-to-all-done
  24.0 0.5 broadcast.51
  24.5 0.7 reduce.10
  25.3 2.6 convolution_convert_fusion.1
  28.0 0.6 copy.77
  28.5 48.2 %all_to_all.16 = bf16[32,2,32,896]{3,2,1,0:T(8,128)(2,1)S(1)} all-to-all(bf16[32,2,32,896]{3,2,1,0:T(8,128)(2,1)S(1)} %bitcast.133), channel_id=1, replica_groups=mesh['dp'=32,'db'=4] {'dp'}, dimensions={0} | all-to-all | bytes 7340032 | tf_op jit(solution)/shard_map/all_to_all | solution.py:93
  76.8 1.4 copy.78
  78.2 0.7 convolution_convert_fusion.2
  79.1 3.5 collective-permute-start
  82.6 1.3 collective-permute-start.1
  84.1 0.9 collective-permute-done
  85.0 4.3 collective-permute-done.1
  89.2 1.8 fusion.36
  91.3 1.6 copy.81
  92.9 2.6 copy.84
  95.5 42.6 %all-gather.5.cloned.1.call-done = bf16[18,128,896]{2,1,0:T(8,128)(2,1)} async-done(((bf16[18,32,896]{2,1,0:T(8,128)(2,1)}), bf16[18,128,896]{2,1,0:T(8,128)(2,1)}) %all-gather.5.cloned.1.call-update) | async-done | bytes 4128784 | tf_op jit(solution)/shard_map/all_gather | solution.py:100
  138.1 7.4 %fusion.33 = bf16[288,8,8,128]{3,1,2,0:T(8,128)(2,1)S(1)} fusion(bf16[2304,896]{1,0:T(8,128)(2,1)} %bitcast.161, bf16[896,1024]{1,0:T(8,128)(2,1)S(1)} %copy-done), kind=kOutput, calls=%fused_computation.50 | convolution fusion | flops 4230217728 | bytes 10682368 | tf_op jit(solution)/shard_map/dot_general | solution.py:102
  145.6 1.3 copy.80
  146.9 0.9 copy-done.16
  147.8 0.6 copy-done.17
  148.3 5.5 %fusion.32 = bf16[288,8,8,128]{3,1,2,0:T(8,128)(2,1)S(1)} fusion(bf16[2304,896]{1,0:T(8,128)(2,1)S(1)} %bitcast.164, bf16[896,1024]{1,0:T(8,128)(2,1)S(1)} %copy-done.17), kind=kOutput, calls=%fused_computation.49 | convolution fusion | flops 4230217728 | bytes 10682368 | tf_op jit(solution)/shard_map/dot_general | solution.py:103
  153.8 3.4 copy.82
  157.2 1.8 fusion.23
  158.9 3.6 fusion.82
  162.5 15.7 %convert_bitcast_fusion = bf16[9,256,8,128]{3,1,2,0:T(8,128)(2,1)} fusion(bf16[9,64,8,128]{3,2,1,0:T(8,128)(2,1)} %bitcast.159, f32[9,8,64]{2,1,0:T(8,128)S(1)} %get-tuple-element.43, f32[9,8,256,64]{2,3,1,0:T(8,128)} %copy-done.5), kind=kOutput, calls=%fused_computation.23 | convolution fusion | flops 310252288 | bytes 10635264 | tf_op jit(solution)/shard_map/chqk,cqhd->ckhd/dot_general | solution.py:124
  178.2 5.7 %copy.72 = bf16[9,256,8,128]{3,2,1,0:T(8,128)(2,1)S(1)} copy(bf16[9,256,8,128]{3,1,2,0:T(8,128)(2,1)} %convert_bitcast_fusion) | data formatting | bytes 9437184 | tf_op jit(solution)/shard_map/convert_element_type | solution.py:126
  184.0 5.8 %fusion.8 = (f32[9,8,64]{2,1,0:T(8,128)S(1)}, f32[9,8,256,64]{2,3,1,0:T(8,128)S(1)}) fusion(f32[9,8,64,256]{3,2,1,0:T(8,128)S(1)} %copy-done.4, f32[9,8,64]{2,1,0:T(8,128)S(1)} %get-tuple-element.43, bf16[9,64,8,128]{3,2,1,0:T(8,128)(2,1)S(1)} %bitcast.160, bf16[9,256,8,128]{3,2,1,0:T(8,128)(2,1)} %bitcast.148), kind=kOutput, calls=%fused_computation.16 | convolution fusion | flops 305524224 | bytes 15372288 | tf_op jit(solution)/shard_map/cqhd,ckhd->chqk/dot_general | solution.py:121
  189.8 1.5 fusion.10
  191.3 1.4 copy-done.3
  192.7 1.7 convert_bitcast_fusion.1
  194.4 3.3 copy.70
  197.7 7.3 %fusion.6 = f32[2304,896]{1,0:T(8,128)} fusion(bf16[896,1024]{1,0:T(8,128)(2,1)S(1)} %copy-done, bf16[288,8,8,128]{3,2,1,0:T(8,128)(2,1)S(1)} %bitcast.152), kind=kOutput, calls=%fused_computation.12 | convolution fusion | flops 4227858432 | bytes 14811136 | tf_op jit(solution)/shard_map/nf,ef->ne/dot_general | solution.py:141
  205.0 9.5 %convolution_add_fusion = f32[2304,896]{1,0:T(8,128)} fusion(f32[2304,896]{1,0:T(8,128)} %fusion.6, bf16[896,1024]{1,0:T(8,128)(2,1)S(1)} %copy-done.18, bf16[288,8,8,128]{3,2,1,0:T(8,128)(2,1)S(1)} %bitcast.150), kind=kOutput, calls=%fused_computation.4 | convolution fusion | flops 4229922816 | bytes 23068672 | tf_op jit(solution)/shard_map/nf,ef->ne/dot_general | solution.py:142
  214.5 79.9 %reduce-scatter.2.cloned.1.call-done = f32[18,32,896]{2,1,0:T(8,128)} async-done(((f32[18,128,896]{2,1,0:T(8,128)}), f32[18,32,896]{2,1,0:T(8,128)}) %reduce-scatter.2.cloned.1.call-update) | async-done | bytes 2064400 | tf_op jit(solution)/shard_map/reduce_scatter | solution.py:146
  294.3 1.3 fusion.80
  295.6 1.3 collective-permute-start.2
  296.9 4.5 collective-permute-start.3
  301.5 0.3 collective-permute-done.2
  301.8 1.6 collective-permute-done.3
  303.4 6.4 %fusion.37 = (f32[896]{0:T(1024)S(1)}, f32[896]{0:T(1024)S(1)}, f32[896]{0:T(1024)S(1)}, bf16[18,32,896]{2,1,0:T(8,128)(2,1)}) fusion(f32[18,32,896]{2,1,0:T(8,128)} %reduce-scatter.2.cloned.1.call-done, bf16[18,32,896]{2,1,0:T(8,128)(2,1)S(1)} %copy-done.7, bf16[18,1,896]{2,1,0:T(2,128)(2,1)S(1)} %collective-permute-done, ...), kind=kLoop, calls=%fused_computation.54 | loop fusion | flops 11867520 | bytes 5376000 | tf_op jit(solution)/shard_map/reduce_sum | solution.py:49
  309.8 0.6 maximum_bitcast_fusion
  310.4 10.0 %fusion.4 = f32[896,1024]{1,0:T(8,128)} fusion(bf16[2304,896]{1,0:T(8,128)(2,1)} %bitcast.162, bf16[288,8,8,128]{3,2,1,0:T(8,128)(2,1)} %bitcast.153), kind=kOutput, calls=%fused_computation.10 | convolution fusion | flops 4227858432 | bytes 12517376 | tf_op jit(solution)/shard_map/ne,nf->ef/dot_general | solution.py:137
  320.5 0.4 copy.88
  320.9 1.2 convolution_convert_fusion
  322.2 2.4 copy.89
  324.6 7.6 %all-to-all-start.2 = ((bf16[32,2,32,896]{3,2,1,0:T(8,128)(2,1)}), bf16[32,2,32,896]{3,2,1,0:T(8,128)(2,1)}, u32[]{:S(2)}, u32[]{:S(2)}) async-start(bf16[32,2,32,896]{3,2,1,0:T(8,128)(2,1)} %bitcast.132), calls=%async_computation.3 | async-start | bytes 7340032 | tf_op jit(solution)/shard_map/all_to_all | solution.py:155
  332.4 9.9 %fusion.1 = f32[896,1024]{1,0:T(8,128)} fusion(bf16[2304,896]{1,0:T(8,128)(2,1)} %bitcast.163, bf16[288,8,8,128]{3,2,1,0:T(8,128)(2,1)} %bitcast.151), kind=kOutput, calls=%fused_computation.7 | convolution fusion | flops 4227858432 | bytes 12517376 | tf_op jit(solution)/shard_map/ne,nf->ef/dot_general | solution.py:138
  342.3 3.8 fusion.54
  346.2 0.8 copy.68
  347.0 13.3 %fusion.51 = bf16[9,64,8,128]{3,1,2,0:T(8,128)(2,1)S(1)} fusion(bf16[9,256,8,128]{3,2,1,0:T(8,128)(2,1)} %bitcast.149, f32[9,8,64]{2,1,0:T(8,128)S(1)} %get-tuple-element.43, f32[9,8,256,64]{2,3,1,0:T(8,128)} %copy-done.5), kind=kOutput, calls=%fused_computation.66 | convolution fusion | flops 308482816 | bytes 10635264 | tf_op jit(solution)/shard_map/chqk,ckhd->cqhd/dot_general | solution.py:118
  360.3 1.0 copy.64
  361.3 2.0 copy_bitcast_fusion
  363.3 33.0 %all-gather.7.cloned.1.call-done = f32[128,3,896]{2,1,0:T(4,128)} async-done(((f32[1,3,896]{2,1,0:T(4,128)}), f32[128,3,896]{2,1,0:T(4,128)}) %all-gather.7.cloned.1.call-update) | async-done | bytes 1376272 | tf_op jit(solution)/shard_map/all_gather | solution.py:167
  396.3 2.4 reduce_sum.79
  398.7 4.3 fusion.26
  403.1 4.0 copy.74
  407.0 111.9 %all-reduce.3.cloned.1.call-done = (f32[896,1024]{1,0:T(8,128)}, f32[896,1024]{1,0:T(8,128)}) async-done(((f32[896,1024]{1,0:T(8,128)}, f32[896,1024]{1,0:T(8,128)}), (f32[896,1024]{1,0:T(8,128)}, f32[896,1024]{1,0:T(8,128)})) %all-reduce.3.cloned.1.call-update) | async-done | bytes 7340048 | tf_op jit(solution)/shard_map/psum | solution.py:166
  518.9 4.5 copy.146
  523.4 1.8 copy.147
  (60 shorter events, 1.8 us)
Async XLA Ops:
  7.2 131.0 %copy-start = (bf16[896,1024]{1,0:T(8,128)(2,1)S(1)}, bf16[896,1024]{1,0:T(8,128)(2,1)}, u32[]{:S(2)}) copy-start(bf16[896,1024]{1,0:T(8,128)(2,1)} %param.11) | copy-start | bytes 5505028
  10.1 13.9 %all-to-all-start = ((s32[32,1,2]{2,1,0:T(1,128)}), s32[32,1,2]{2,1,0:T(1,128)S(1)}, u32[]{:S(2)}, u32[]{:S(2)}) async-start(s32[32,1,2]{2,1,0:T(1,128)} %bitcast), calls=%async_computation | async-start | bytes 32768 | tf_op jit(solution)/shard_map/all_to_all | solution.py:84
  18.5 119.6 %all-gather.5.cloned.1.call-start = ((), (), s32[]{:S(2)}) async-start(), calls=%async_computation.4 | async-start | bytes 5160960 | tf_op jit(solution)/shard_map/all_gather | solution.py:100
  78.1 5.8 %copy-start.15 = (f32[3,896]{1,0:T(4,128)S(1)}, f32[3,896]{1,0:T(4,128)}, u32[]{:S(2)}) copy-start(f32[3,896]{1,0:T(4,128)} %param.13) | copy-start | bytes 32260
  79.0 5.0 copy-start.8
  79.1 5.9 %collective-permute-start = (bf16[18,1,896]{2,1,0:T(2,128)(2,1)S(1)}, bf16[18,1,896]{2,1,0:T(2,128)(2,1)S(1)}, u32[]{:S(2)}, u32[]{:S(2)}) collective-permute-start(bf16[18,1,896]{2,1,0:T(2,128)(2,1)S(1)} %get-tuple-element.41), channel_id=1, source_target_pairs={{0,1},{1,2},{2,3},{4,5},{5,6},{6,7},{8,9},{9,10},{10,11},{12,13},{... | collective-permute-start | bytes 96776 | tf_op jit(solution)/shard_map/ppermute | solution.py:20
  82.6 6.6 %collective-permute-start.1 = (bf16[18,1,896]{2,1,0:T(2,128)(2,1)S(1)}, bf16[18,1,896]{2,1,0:T(2,128)(2,1)S(1)}, u32[]{:S(2)}, u32[]{:S(2)}) collective-permute-start(bf16[18,1,896]{2,1,0:T(2,128)(2,1)S(1)} %get-tuple-element.42), channel_id=1, source_target_pairs={{1,0},{2,1},{3,2},{5,4},{6,5},{7,6},{9,8},{10,9},{11,10},{13,12},{... | collective-permute-start | bytes 96776 | tf_op jit(solution)/shard_map/ppermute | solution.py:23
  84.1 5.2 copy-start.6
  91.1 203.2 %reduce-scatter.2.cloned.1.call-start = ((), (), s32[]{:S(2)}) async-start(), calls=%async_computation.5 | async-start | bytes 10321920 | tf_op jit(solution)/shard_map/reduce_scatter | solution.py:146
  145.6 2.2 copy-start.16
  145.6 2.7 copy-start.17
  148.3 8.8 %copy-start.2 = (bf16[288,8,8,128]{3,2,1,0:T(8,128)(2,1)}, bf16[288,8,8,128]{3,2,1,0:T(8,128)(2,1)S(1)}, u32[]{:S(2)}) copy-start(bf16[288,8,8,128]{3,2,1,0:T(8,128)(2,1)S(1)} %copy.80) | copy-start | bytes 14155780
  158.9 3.6 copy-start.5
  178.2 5.8 %copy-start.4 = (f32[9,8,64,256]{3,2,1,0:T(8,128)S(1)}, f32[9,8,64,256]{3,2,1,0:T(8,128)}, u32[]{:S(2)}) copy-start(f32[9,8,64,256]{3,2,1,0:T(8,128)} %get-tuple-element.44) | copy-start | bytes 14155780
  178.2 5.8 %copy-start.14 = (bf16[72,8,8,128]{3,2,1,0:T(8,128)(2,1)S(1)}, bf16[72,8,8,128]{3,2,1,0:T(8,128)(2,1)}, u32[]{:S(2)}) copy-start(bf16[72,8,8,128]{3,2,1,0:T(8,128)(2,1)} %copy.84) | copy-start | bytes 3538948
  183.9 21.0 %copy-start.10 = (bf16[9,256,8,128]{3,2,1,0:T(8,128)(2,1)}, bf16[9,256,8,128]{3,2,1,0:T(8,128)(2,1)S(1)}, u32[]{:S(2)}) copy-start(bf16[9,256,8,128]{3,2,1,0:T(8,128)(2,1)S(1)} %copy.72) | copy-start | bytes 14155780
  191.3 1.4 copy-start.3
  197.6 7.3 %copy-start.11 = (bf16[9,256,8,128]{3,2,1,0:T(8,128)(2,1)}, bf16[9,256,8,128]{3,2,1,0:T(8,128)(2,1)S(1)}, u32[]{:S(2)}) copy-start(bf16[9,256,8,128]{3,2,1,0:T(8,128)(2,1)S(1)} %copy.70) | copy-start | bytes 14155780
  197.7 7.3 %copy-start.18 = (bf16[896,1024]{1,0:T(8,128)(2,1)S(1)}, bf16[896,1024]{1,0:T(8,128)(2,1)}, u32[]{:S(2)}) copy-start(bf16[896,1024]{1,0:T(8,128)(2,1)} %param.12) | copy-start | bytes 5505028
  214.4 89.0 %copy-start.7 = (bf16[18,32,896]{2,1,0:T(8,128)(2,1)S(1)}, bf16[18,32,896]{2,1,0:T(8,128)(2,1)}, u32[]{:S(2)}) copy-start(bf16[18,32,896]{2,1,0:T(8,128)(2,1)} %copy-done.6) | copy-start | bytes 3096580
  214.4 89.0 %copy-start.9 = (bf16[3,8,32,896]{3,2,1,0:T(8,128)(2,1)S(1)}, bf16[3,8,32,896]{3,2,1,0:T(8,128)(2,1)}, u32[]{:S(2)}) copy-start(bf16[3,8,32,896]{3,2,1,0:T(8,128)(2,1)} %copy-done.8) | copy-start | bytes 4128772
  214.4 181.9 %all-gather.7.cloned.1.call-start = ((), (), s32[]{:S(2)}) async-start(), calls=%async_computation.6 | async-start | bytes 1849344 | tf_op jit(solution)/shard_map/all_gather | solution.py:167
  295.6 6.1 %collective-permute-start.2 = (f32[18,1,896]{2,1,0:T(1,128)S(1)}, f32[18,1,896]{2,1,0:T(1,128)S(1)}, u32[]{:S(2)}, u32[]{:S(2)}) collective-permute-start(f32[18,1,896]{2,1,0:T(1,128)S(1)} %get-tuple-element.39), channel_id=1, source_target_pairs={{1,0},{2,1},{3,2},{5,4},{6,5},{7,6},{9,8},{10,9},{11,10},{13,12},{... | collective-permute-start | bytes 193544 | tf_op jit(solution)/shard_map/ppermute | solution.py:23
  296.9 6.4 %collective-permute-start.3 = (f32[18,1,896]{2,1,0:T(1,128)S(1)}, f32[18,1,896]{2,1,0:T(1,128)S(1)}, u32[]{:S(2)}, u32[]{:S(2)}) collective-permute-start(f32[18,1,896]{2,1,0:T(1,128)S(1)} %get-tuple-element.40), channel_id=1, source_target_pairs={{0,1},{1,2},{2,3},{4,5},{5,6},{6,7},{8,9},{9,10},{10,11},{12,13},{... | collective-permute-start | bytes 193544 | tf_op jit(solution)/shard_map/ppermute | solution.py:20
  310.4 10.0 %copy-start.12 = (bf16[18,32,896]{2,1,0:T(8,128)(2,1)S(1)}, bf16[18,32,896]{2,1,0:T(8,128)(2,1)}, u32[]{:S(2)}) copy-start(bf16[18,32,896]{2,1,0:T(8,128)(2,1)} %get-tuple-element.38) | copy-start | bytes 3096580
  324.6 74.1 %all-to-all-start.2 = ((bf16[32,2,32,896]{3,2,1,0:T(8,128)(2,1)}), bf16[32,2,32,896]{3,2,1,0:T(8,128)(2,1)}, u32[]{:S(2)}, u32[]{:S(2)}) async-start(bf16[32,2,32,896]{3,2,1,0:T(8,128)(2,1)} %bitcast.132), calls=%async_computation.3 | async-start | bytes 7340032 | tf_op jit(solution)/shard_map/all_to_all | solution.py:155
  332.2 186.7 %all-reduce.3.cloned.1.call-start = ((), (), s32[]{:S(2)}) async-start(), calls=%async_computation.7 | async-start | bytes 14680064 | tf_op jit(solution)/shard_map/psum | solution.py:166
  518.9 4.5 copy-start.13
  518.9 6.4 %copy-start.1 = (bf16[896,1024]{1,0:T(8,128)(2,1)S(1)}, bf16[896,1024]{1,0:T(8,128)(2,1)}, u32[]{:S(2)}) copy-start(bf16[896,1024]{1,0:T(8,128)(2,1)} %param.11) | copy-start | bytes 5505028
Sparse Core Ops, SparseCore 0:
  91.2 46.8 all-gather.4
  214.6 79.7 reduce-scatter.1
  310.5 85.7 all-gather.6
  400.6 118.1 all-reduce.2
